TPU v7x, 128 devices: a whole 4x4x4 slice. The times are simulated.
128 devices in a mesh: wide: 64 (over z, y, x_hi, core), narrow: 2 (over x_lo).
Axes of the slice: x: 4 (x_hi: 2, x_lo: 2; x = x_hi * 2 + x_lo), y: 4, z: 4, core: 2. Of those that a mesh axis runs over, the one named last changes fastest.
Arguments:
- layer_in: bfloat16 [8192, 1536], P('wide'), may hold values from -16 to 16
- lengths: int32 [4], replicated, may hold values from 1 to 8127, as said below
- norm_attn: float32 [1536], replicated, may hold values from 0.1 to 1.9
- w_qkv: bfloat16 [1536, 2048], P(None, 'narrow'), may hold values from -0.15625 to 0.15625
- qkv_bias: float32 [2, 1024], P('narrow'), may hold values from -3 to 3
- w_out: bfloat16 [1536, 1536], P('narrow'), may hold values from -4 to 4
- norm_mlp: float32 [1536], replicated, may hold values from 0.1 to 1.9
- w_gate: bfloat16 [1536, 8960], P(None, 'narrow'), may hold values from -0.15625 to 0.15625
- w_up: bfloat16 [1536, 8960], P(None, 'narrow'), may hold values from -0.15625 to 0.15625
- w_down: bfloat16 [8960, 1536], P('narrow'), may hold values from -0.0625 to 0.0625
- out_grad: bfloat16 [8192, 1536], P('wide'), may hold values from -16 to 16
Outputs:
- layer_out: bfloat16 [8192, 1536], P('wide')
- in_grad: bfloat16 [8192, 1536], P('wide')
- grad_norm_attn: float32 [1536], P('wide')
- grad_qkv: float32 [1536, 2048], P('wide', 'narrow')
- grad_bias: float32 [2, 7, 128], P('narrow', None, 'wide')
- grad_value_bias: float32 [2, 128], P('narrow', 'wide')
- grad_out: float32 [1536, 1536], P('narrow', 'wide')
- grad_norm_mlp: float32 [1536], P('wide')
- grad_gate: float32 [1536, 8960], P('wide', 'narrow')
- grad_up: float32 [1536, 8960], P('wide', 'narrow')
- grad_down: float32 [8960, 1536], P('narrow', 'wide')
Inputs may be any that keep to these rules, and one draw needn't show every extreme that they name: 4 sequences packed one after another; their lengths sum to 8192; one of them, which one is drawn, reaches from the first token shard of wide to the last.
All inputs are finite; a program needn't handle non-finite values.
Results may differ from a plain program's by a relative error of at most 0.022.
Values may be sent and summed in bfloat16 or wider, within the bound.
A program may use at most 384 MiB of HBM per device.

v0:
```python
import functools
import math

import jax
import jax.numpy as jnp
import numpy as np
from jax import lax
from jax.experimental import pallas as pl
from jax.experimental.pallas import tpu as pltpu
from jax.sharding import Mesh
from jax.sharding import PartitionSpec as P

HD = 128
QH = 12
KVH = 2
HEADS = QH // KVH
D = 1536
FF = 8960
TOK = 128
TOKENS = 8192
SEQS = 4
NQ = HEADS * TOK
GROUP = 8
UNITS = FF // 2 // GROUP
WINDOW = 768
COLUMNS = 640

AXES = ("z", "y", "xh", "c", "n")
SIZE = {"z": 4, "y": 4, "xh": 2, "c": 2, "n": 2}
WIDE = ("z", "y", "xh", "c")
MESH = pl.DeviceIdType.MESH

rms_eps = 1e-06
rope_base = 10000.0
big_negative = -1e30
SCALE = HD ** (-0.5)
SCALE_LOG2 = SCALE * math.log2(math.e)
KEY_BLOCK = 512
BLOCK_SHARDS = KEY_BLOCK // TOK
Q_CHUNK = 256

bf16 = jnp.bfloat16
f32 = jnp.float32
VMEM = pl.BlockSpec(memory_space=pltpu.VMEM)
SMEM = pl.BlockSpec(memory_space=pltpu.SMEM)
ANY = pl.BlockSpec(memory_space=pl.ANY)


def nn(a, b):
    return lax.dot_general(a, b, (((1,), (0,)), ((), ())), preferred_element_type=f32)


def nt(a, b):
    return lax.dot_general(a, b, (((1,), (1,)), ((), ())), preferred_element_type=f32)


def tn(a, b):
    return lax.dot_general(a, b, (((0,), (0,)), ((), ())), preferred_element_type=f32)


def here():
    return {a: lax.axis_index(a) for a in AXES}


def step(me, axis, by):
    return lax.rem(me[axis] + by, SIZE[axis])


def at(me, **moved):
    return tuple(step(me, a, moved[a]) if a in moved else me[a] for a in AXES)


def sequence_starts(ids, lengths):
    starts, end = jnp.zeros_like(ids), 0
    for s in range(SEQS):
        end = end + lengths[s]
        starts = starts + jnp.where(ids >= end, lengths[s], 0)
    return starts


def token_rows(me, lengths):
    column = lax.broadcasted_iota(jnp.int32, (1, 2 * NQ), 1)
    ids = shard_of(me) // 2 * (2 * TOK) + column // NQ * TOK + column % TOK
    return ids, sequence_starts(ids, lengths)


def hail(peers):
    barrier = pltpu.get_barrier_semaphore()
    for p in peers:
        pl.semaphore_signal(barrier, inc=1, device_id=p, device_id_type=MESH)
    return lambda: pl.semaphore_wait(barrier, len(peers))


def greet(peers):
    hail(peers)()


class Copies:
    def __init__(self, send_sems, recv_sems):
        self.send_sems, self.recv_sems, self.used, self.started = send_sems, recv_sems, 0, []

    def make(self, src, dst, target):
        self.used += 1
        return self.numbered(self.used - 1, src, dst, target)

    def numbered(self, k, src, dst, target):
        return pltpu.make_async_remote_copy(
            src_ref=src,
            dst_ref=dst,
            send_sem=self.send_sems.at[k],
            recv_sem=self.recv_sems.at[k],
            device_id=target,
            device_id_type=MESH,
        )

    def send(self, src, dst, target):
        copy = self.make(src, dst, target)
        copy.start()
        self.started.append(copy)
        return copy

    def finish(self):
        for copy in self.started:
            copy.wait_send()


class Moves:
    def __init__(self, move_sems):
        self.move_sems, self.started = move_sems, []

    def start(self, src, dst):
        copy = pltpu.make_async_copy(src, dst, self.move_sems.at[len(self.started)])
        copy.start()
        self.started.append(copy)
        return copy

    def finish(self, copies):
        for copy in copies:
            copy.wait()


def sems(count):
    return [pltpu.SemaphoreType.DMA((count,)), pltpu.SemaphoreType.DMA((count,))]


def params(ident, mib=60):
    return pltpu.CompilerParams(
        collective_id=ident, has_side_effects=True, vmem_limit_bytes=mib * 2**20
    )


def whole_tiles(values):
    pad = jnp.zeros((values.shape[0], COLUMNS - values.shape[1]), values.dtype)
    return jnp.concatenate([values, pad], axis=1)


def three(ref):
    return ref[0].astype(f32) + ref[1].astype(f32) + ref[2].astype(f32)


def shard_of(me):
    return ((me["z"] * 4 + me["y"]) * 2 + me["xh"]) * 2 + me["c"]


class Rows:
    def __init__(self, me, copies, source, slots):
        self.me, self.copies, self.source, self.slots = me, copies, source, slots
        half = TOK // 2
        n = me["n"]
        self.mine = pl.ds(pl.multiple_of(half * n, half), half)
        self.theirs = pl.ds(pl.multiple_of(half * (1 - n), half), half)
        self.own = slots.at[me["y"], me["c"]]
        self.near, self.far, self.across = [], {}, {}

    def pair(self):
        self.near.append(self.copies.send(self.source, self.own, at(self.me, c=1)))

    def slot(self, d, rows):
        return self.slots.at[lax.rem(self.me["y"] + (4 - d), 4), self.me["c"], rows]

    def start(self, *steps):
        for d in steps:
            self.far[d] = self.copies.send(
                self.source.at[self.mine], self.own.at[self.mine], at(self.me, y=d)
            )

    def pass_on(self, *steps):
        for d in steps:
            self.far[d].wait_recv()
            got = self.slot(d, self.mine)
            self.across[d] = self.copies.send(got, got, at(self.me, n=1))
            self.near.append(self.copies.send(got, got, at(self.me, c=1)))

    def complete(self, *steps):
        for d in steps:
            self.across[d].wait_recv()
            got = self.slot(d, self.theirs)
            self.near.append(self.copies.send(got, got, at(self.me, c=1)))

    def wait(self):
        for copy in self.near:
            copy.wait_recv()


def attend_kernel(
    lengths, x, gain, bias, freqs, og, w_qkv_hbm, w_out_hbm, w_gate_hbm, w_up_hbm,
    kv_hbm, q_hbm, act_hbm, resid_hbm, exact_hbm, lse_hbm, rope_hbm, gate_hbm, up_hbm, og_all, al_all,
    stats, acc, low_acc, stats_in, acc_in, low_in, w_qkv, w_out, o, pa, pb,
    kv, q, act, resid, exact, lse, rope, gate_w, up_w, wide_gate, wide_up, send_sems, recv_sems, local_sems,
):
    me = here()
    moves, kept_back = Moves(local_sems), []
    load_w = moves.start(w_qkv_hbm, w_qkv)
    ids, start = token_rows(me, lengths)
    z, y, xh, c = me["z"], me["y"], me["xh"], me["c"]
    partner, across, other = at(me, c=1), at(me, xh=1), at(me, n=1)
    ys = {d: at(me, y=d) for d in (1, 2, 3)}
    zs = {d: at(me, z=d) for d in (1, 2, 3)}
    everyone_in = hail([partner, across, other, *ys.values(), *zs.values()])
    rows = x[...].astype(f32)
    inverse = lax.rsqrt(jnp.mean(rows * rows, axis=-1, keepdims=True) + rms_eps)
    act[...] = (rows * inverse * gain[...].reshape(1, D)).astype(bf16)
    token = shard_of(me) * TOK + lax.broadcasted_iota(jnp.int32, (TOK, 1), 0)
    angles = (token - sequence_starts(token, lengths)).astype(f32) * freqs[...]
    cosine = jnp.cos(angles)
    turned = jnp.sin(angles)
    first_half = lax.broadcasted_iota(jnp.int32, (TOK, HD), 1) < HD // 2
    sine = jnp.where(first_half, -turned, turned)
    rope[0], rope[1] = cosine, sine
    kept_back.append(moves.start(rope, rope_hbm))
    front = HEADS * HD

    def turn(values):
        return values * cosine + pltpu.roll(values, HD // 2, 1) * sine

    load_w.wait()
    back = nn(act[...], w_qkv[:, front:]) + bias[:, front:]
    mine = kv.at[z, y, xh]
    mine[:, pl.ds(0, HD)] = turn(back[:, :HD]).astype(bf16)
    mine[:, pl.ds(HD, HD)] = back[:, HD:].astype(bf16)
    everyone_in()
    kept_back.append(moves.start(act, act_hbm))
    load_out = moves.start(w_out_hbm, w_out)
    copies = Copies(send_sems, recv_sems)
    rows_of_og = Rows(me, copies, og, og_all)
    rows_of_og.start(1, 3)
    first = copies.send(mine, mine, across)
    ahead = nn(act[...], w_qkv[:, :front]) + bias[:, :front]
    for h in range(HEADS):
        head = turn(ahead[:, h * HD : (h + 1) * HD]).astype(bf16)
        q[c, pl.ds(h * TOK, TOK), :] = head
    share_q = copies.send(q.at[c], q.at[c], partner)
    rows_of_og.pair()
    kept_back.append(moves.start(og, og_all.at[y, c]))
    stats[:, 0:1, :] = jnp.full((2, 1, NQ), big_negative, f32)
    stats[:, 1:8, :] = jnp.zeros((2, 7, NQ), f32)
    acc[...] = jnp.zeros_like(acc)
    low_acc[...] = jnp.zeros_like(low_acc)
    last = shard_of(me) // BLOCK_SHARDS
    kept = start < last * KEY_BLOCK
    half = TOK // 2
    keys_here = 2 * half

    def take(parts, masked):
        def both(columns):
            return jnp.concatenate(
                [
                    kv[zi, yi, :, pl.ds(pl.multiple_of(half * k, half), half), columns].reshape(
                        keys_here, HD
                    )
                    for zi, yi, k in parts
                ],
                axis=0,
            )

        keys, values = both(pl.ds(0, HD)), both(pl.ds(HD, HD)).T
        for chunk in range(2 * NQ // Q_CHUNK):
            core, cs = divmod(chunk * Q_CHUNK, NQ)
            cs = pl.ds(cs, Q_CHUNK)
            here_cols = slice(chunk * Q_CHUNK, (chunk + 1) * Q_CHUNK)
            scores = nt(keys, q[core, cs, :]) * SCALE_LOG2
            if masked:
                ((zi, yi, k),) = parts
                place = lax.broadcasted_iota(jnp.int32, (keys_here, Q_CHUNK), 0)
                first_key = (4 * zi + yi) * KEY_BLOCK + c * TOK + half * k
                key_ids = first_key + place + place // half * (2 * TOK - half)
                allowed = (key_ids >= start[:, here_cols]) & (key_ids <= ids[:, here_cols])
                scores = jnp.where(allowed, scores, big_negative)
            old = stats[core, 0:1, cs]
            new = jnp.maximum(old, jnp.max(scores, axis=0, keepdims=True))
            if masked:
                probs = jnp.where(allowed, jnp.exp2(scores - new), 0.0)
            else:
                taken = kept[:, here_cols]
                new = jnp.where(taken, new, old)
                probs = jnp.exp2(scores - jnp.where(taken, new, -big_negative))
            fade = jnp.exp2(old - new)
            stats[core, 0:1, cs] = new
            stats[core, 1:2, cs] = stats[core, 1:2, cs] * fade + jnp.sum(probs, axis=0, keepdims=True)
            upper = probs.astype(bf16)
            rest = (probs - upper.astype(f32)).astype(bf16)
            acc[core, :, cs] = acc[core, :, cs] * fade + nn(values, upper)
            low_acc[core, :, cs] = low_acc[core, :, cs] * fade + nn(values, rest)

    def pair(za, ya, zb, yb):
        a, b = 4 * za + ya, 4 * zb + yb
        inner = (jnp.minimum(a, b) > 0) & (jnp.maximum(a, b) < last)

        @pl.when(inner)
        def _():
            take([(za, ya, 0), (zb, yb, 1)], False)

        @pl.when(jnp.logical_not(inner))
        def _():
            @pl.loop(0, 2)
            def _(k):
                zi, yi = jnp.where(k == 0, za, zb), jnp.where(k == 0, ya, yb)
                index = 4 * zi + yi
                edge = (index == 0) | (index == last)

                @pl.when(edge & (index <= last))
                def _():
                    take([(zi, yi, k)], True)

                @pl.when((index < last) & jnp.logical_not(edge))
                def _():
                    take([(zi, yi, k)], False)

    first.wait_recv()
    low, high = pl.ds(0, half), pl.ds(half, half)

    def slot(zi, yi, rows):
        return kv.at[zi, yi, :, rows]

    def before(axis, d):
        return lax.rem(me[axis] + (4 - d), 4)

    first_low, first_high = {}, {}
    for d in (1, 3, 2):
        first_low[d] = copies.send(slot(z, y, low), slot(z, y, low), ys[d])
        first_high[d] = copies.send(slot(z, y, high), slot(z, y, high), zs[d])
    share_q.wait_recv()

    kept_back.append(moves.start(q, q_hbm))
    first_unit = (y * 2 + c) * UNITS
    tile = jnp.minimum(first_unit // 128, FF // 2 // 128 - WINDOW // 128)
    window = pl.ds(pl.multiple_of(tile * 128, 128), WINDOW)
    load_gate = moves.start(w_gate_hbm.at[:, window], wide_gate)
    load_up = moves.start(w_up_hbm.at[:, window], wide_up)
    pair(z, y, z, y)
    second_from = copies.used
    copies.used += 24
    for i, e in enumerate((0, 1, 3, 2)):
        yi, zi = before("y", e), before("z", e)
        if e:
            first_low[e].wait_recv()
            first_high[e].wait_recv()
        for j, d in enumerate((1, 3, 2)):
            k = second_from + 2 * (3 * i + j)
            for copy in (
                copies.numbered(k, slot(z, yi, low), slot(z, yi, low), zs[d]),
                copies.numbered(k + 1, slot(zi, y, high), slot(zi, y, high), ys[d]),
            ):
                copy.start()
                copies.started.append(copy)
    rows_of_og.start(2)
    rows_of_og.pass_on(1, 3)

    @pl.loop(1, 4)
    def _(e):
        pair(z, before("y", e), before("z", e), y)

    def places(k):
        i, j = k // 3, lax.rem(k, 3)
        e = jnp.where(i < 2, i, 5 - i)
        d = jnp.where(j < 2, 1 + 2 * j, 2)
        return before("z", d), before("y", e), before("z", e), before("y", d)

    def arrive(k):
        za, ya, zb, yb = places(k)
        one, two = slot(za, ya, low), slot(zb, yb, high)
        copies.numbered(second_from + 2 * k, one, one, zs[1]).wait_recv()
        copies.numbered(second_from + 2 * k + 1, two, two, ys[1]).wait_recv()
        pair(za, ya, zb, yb)

    pl.loop(0, 8)(arrive)
    rows_of_og.pass_on(2)
    pl.loop(8, 12)(arrive)
    kept_back.append(moves.start(kv, kv_hbm))
    merge = [
        copies.send(stats.at[1 - c], stats_in, partner),
        copies.send(acc.at[1 - c], acc_in, partner),
        copies.send(low_acc.at[1 - c], low_in, partner),
    ]
    rows_of_og.complete(1, 3, 2)
    for copy in merge:
        copy.wait_recv()
    own_top, in_top = stats[c, 0:1, :], stats_in[0:1, :]
    top = jnp.maximum(own_top, in_top)
    own_part, in_part = jnp.exp2(own_top - top), jnp.exp2(in_top - top)
    total = stats[c, 1:2, :] * own_part + stats_in[1:2, :] * in_part
    inverse = 1.0 / total
    own_part, in_part = own_part * inverse, in_part * inverse
    rows = acc[c] * own_part + acc_in[...] * in_part
    exact[...] = rows + (low_acc[c] * own_part + low_in[...] * in_part)
    rows = rows.T.astype(bf16)
    for h in range(HEADS):
        o[:, pl.ds(h * HD, HD)] = rows[h * TOK : (h + 1) * TOK]
    load_out.wait()
    pa[...] = nn(o[...], w_out[...]).astype(bf16)
    swap = copies.send(pa, pb, other)
    own_al = al_all.at[y]
    al_moves = {d: copies.send(o, own_al, ys[d]) for d in (1, 3, 2)}
    kept_back.append(moves.start(o, own_al))
    lse[...] = top + jnp.log2(total)
    kept_back.append(moves.start(lse, lse_hbm))
    kept_back.append(moves.start(exact, exact_hbm))
    shift = lax.rem(WINDOW - (first_unit - tile * 128), WINDOW)
    for load, part, weights, whole in (
        (load_gate, wide_gate, gate_w, gate_hbm),
        (load_up, wide_up, up_w, up_hbm),
    ):
        load.wait()

        @pl.loop(0, D // 128)
        def _(index, part=part, weights=weights):
            rows = pl.ds(pl.multiple_of(index * 128, 128), 128)
            rolled = pltpu.roll(part[rows, :].astype(f32), shift, 1)
            weights[rows, :] = rolled[:, :COLUMNS].astype(bf16)

        kept_back.append(moves.start(weights, whole))
    rows_of_og.wait()
    swap.wait_recv()
    resid[...] = x[...].astype(f32) + (pa[...].astype(f32) + pb[...].astype(f32))
    kept_back.append(moves.start(resid, resid_hbm))
    for copy in al_moves.values():
        copy.wait_recv()
    moves.finish(kept_back)
    copies.finish()


def attend(*arrays):
    state = [
        jax.ShapeDtypeStruct((4, 4, 2, TOK, 2 * HD), bf16),
        jax.ShapeDtypeStruct((2, NQ, HD), bf16),
        jax.ShapeDtypeStruct((TOK, D), bf16),
        jax.ShapeDtypeStruct((TOK, D), f32),
        jax.ShapeDtypeStruct((HD, NQ), f32),
        jax.ShapeDtypeStruct((1, NQ), f32),
        jax.ShapeDtypeStruct((2, TOK, HD), f32),
        jax.ShapeDtypeStruct((D, COLUMNS), bf16),
        jax.ShapeDtypeStruct((D, COLUMNS), bf16),
    ]
    return pl.pallas_call(
        attend_kernel,
        out_shape=[
            *state,
            jax.ShapeDtypeStruct((4, 2, TOK, D), bf16),
            jax.ShapeDtypeStruct((4, TOK, HEADS * HD), bf16),
        ],
        in_specs=[SMEM] + [VMEM] * 5 + [ANY] * 4,
        out_specs=[ANY] * 11,
        scratch_shapes=[
            pltpu.VMEM((2, 8, NQ), f32),
            pltpu.VMEM((2, HD, NQ), f32),
            pltpu.VMEM((2, HD, NQ), f32),
            pltpu.VMEM((8, NQ), f32),
            pltpu.VMEM((HD, NQ), f32),
            pltpu.VMEM((HD, NQ), f32),
            pltpu.VMEM((D, (HEADS + 2) * HD), bf16),
            pltpu.VMEM((HEADS * HD, D), bf16),
            pltpu.VMEM((TOK, HEADS * HD), bf16),
            *[pltpu.VMEM((TOK, D), bf16)] * 2,
            *[pltpu.VMEM(a.shape, a.dtype) for a in state],
            *[pltpu.VMEM((D, WINDOW), bf16)] * 2,
            *sems(52),
            pltpu.SemaphoreType.DMA((15,)),
        ],
        compiler_params=params(1),
    )(*arrays)


def mlp_kernel(*refs):
    resid, gain, og, aa, w_out_hbm, og_hbm, gate_hbm, up_w_hbm, w_down_hbm = refs[:9]
    back_hbm, grads_hbm, gains_hbm, gate_sum_hbm, near_hbm, far_hbm, up_hbm, down_hbm, aa_all = refs[9:18]
    wd, og_all, act_all, grad_hidden, hidden, ggp, gup, bk, dn, bk_core, dn_core, bk_sent, bk_in = refs[18:31]
    nb, rn, gate_terms, gate_in, gate_w, up_w, up_terms, down_terms, down_sum, dn_in, w_out = refs[31:42]
    grad_resid, grads, gain_terms, gate_sum, down_near, send_sems, recv_sems, local_sems = refs[42:]
    me = here()
    z, y, c = me["z"], me["y"], me["c"]
    partner, other = at(me, c=1), at(me, n=1)
    ys = {d: at(me, y=d) for d in (1, 2, 3)}
    zs = {d: at(me, z=d) for d in (1, 2, 3)}
    everyone_in = hail([partner, other, *ys.values(), *zs.values()])
    moves, kept_back = Moves(local_sems), []
    load_gate, load_up = moves.start(gate_hbm, gate_w), moves.start(up_w_hbm, up_w)
    units = pl.ds(pl.multiple_of((y * 2 + c) * UNITS, 16), UNITS)
    load_down, load_og = moves.start(w_down_hbm.at[units], wd), moves.start(og_hbm, og_all)
    load_out = moves.start(w_out_hbm, w_out)
    kept_back.append(moves.start(aa, aa_all.at[y, c]))
    everyone_in()
    copies = Copies(send_sems, recv_sems)
    half = TOK // 2
    halves = (pl.ds(0, half), pl.ds(half, half))
    gain = gain[...].reshape(1, D)

    def inverse_of(rows):
        return lax.rsqrt(jnp.mean(rows * rows, axis=-1, keepdims=True) + rms_eps)

    own = act_all.at[y, c]
    far, to_core = {}, {0: [], 1: [], 2: [], 3: []}
    for rows in halves:
        total = resid[rows, :]
        act_all[y, c, rows] = (total * inverse_of(total) * gain).astype(bf16)
        to_core[0].append(copies.send(own.at[rows], own.at[rows], partner))
        for d in (1, 3):
            far[d, len(to_core[0]) - 1] = copies.send(own.at[rows], own.at[rows], ys[d])
    load_down.wait()
    load_og.wait()
    pair = (2 * TOK, D)

    def hidden_back(d):
        yi = step(me, "y", d)
        grad_hidden[yi] = nt(og_all[yi].reshape(pair), wd[...])

    hidden_back(0)
    load_gate.wait()
    load_up.wait()
    bk_cores, dn_cores, bk_moves = {}, {}, {}

    def block(d, beside=None):
        yi = step(me, "y", d)
        rows = act_all[yi].reshape(pair)
        gate = nn(rows, gate_w[:, :UNITS])
        up = nn(rows, up_w[:, :UNITS])
        sigmoid = 1.0 / (1.0 + jnp.exp(-gate))
        silu = gate * sigmoid
        grads = grad_hidden[yi]
        hidden[yi] = (silu * up).astype(bf16)
        ggp[yi] = (grads * up * (sigmoid * (1.0 + gate * (1.0 - sigmoid)))).astype(bf16)
        gup[yi] = (grads * silu).astype(bf16)
        if beside is not None:
            pass_block(beside)
        both = nt(ggp[yi], gate_w[:, :UNITS]) + nt(gup[yi], up_w[:, :UNITS])
        bk[yi] = both.astype(bf16).reshape(2, TOK, D)
        bk_cores[d] = copies.send(bk.at[yi, 1 - c], bk_core.at[yi], partner)
    low, high = halves

    def pass_block(d):
        yi = step(me, "y", d)
        bk_cores[d].wait_recv()
        for k, rows in enumerate((low, high)):
            bk_sent[yi, rows] = (
                bk[yi, c, rows].astype(f32) + bk_core[yi, rows].astype(f32)
            ).astype(bf16)
            if d:
                bk_moves[d, k] = copies.send(
                    bk_sent.at[yi, rows], bk_in.at[d - 1, rows], ys[d]
                )

    def down_block(d):
        yi = step(me, "y", d)
        dn[yi] = nn(hidden[yi], wd[...]).astype(bf16).reshape(2, TOK, D)
        dn_cores[d] = copies.send(dn.at[yi, 1 - c], dn_core.at[yi], partner)

    def sum_down(d):
        yi = step(me, "y", d)
        dn_cores[d].wait_recv()
        down_sum[yi] = (dn[yi, c].astype(f32) + dn_core[yi].astype(f32)).astype(bf16)

    for copy in to_core[0]:
        copy.wait_recv()
    block(0)
    for d in (3, 1, 2):
        hidden_back(d)
    relay = {}
    for k, rows in enumerate(halves):
        for d in (1, 3):
            far[d, k].wait_recv()
            got = act_all.at[lax.rem(y + (4 - d), 4), c, rows]
            to_core[4 - d].append(copies.send(got, got, partner))
            if d == 1 + 2 * k:
                relay[d] = copies.send(got, got, ys[d])
    aa_rows = Rows(me, copies, aa, aa_all)
    aa_rows.start(1, 3, 2)
    aa_rows.pair()
    for copy in to_core[3]:
        copy.wait_recv()
    block(3, 0)
    for d, rows in ((1, low), (3, high)):
        relay[d].wait_recv()
        got = act_all.at[step(me, "y", 2), c, rows]
        to_core[2].append(copies.send(got, got, partner))
    for copy in to_core[1]:
        copy.wait_recv()
    block(1, 3)
    for copy in to_core[2]:
        copy.wait_recv()
    block(2, 1)

    everything = (GROUP * TOK, D)
    all_units = (GROUP * TOK, UNITS)
    gate_terms[...] = tn(ggp[...].reshape(all_units), act_all[...].reshape(everything)).astype(bf16)

    def z_cols(d):
        return pl.ds(pl.multiple_of(step(me, "z", d) * 384, 384), 384)

    gate_moves = {
        d: copies.send(gate_terms.at[:, z_cols(d)], gate_in.at[d - 1], zs[d]) for d in (1, 3, 2)
    }
    pass_block(2)
    aa_rows.pass_on(1, 3, 2)
    for d in (1, 3, 2, 0):
        down_block(d)
    up_terms[...] = tn(gup[...].reshape(all_units), act_all[...].reshape(everything)).astype(bf16)
    kept_back.append(moves.start(up_terms, up_hbm))
    for d in range(4):
        sum_down(d)
    swaps_back = []
    for k, rows in enumerate((low, high)):
        back = bk_sent[y, rows].astype(f32)
        for d in (1, 3, 2):
            bk_moves[d, k].wait_recv()
            back = back + bk_in[d - 1, rows].astype(f32)
        nb[rows] = back.astype(bf16)
        swaps_back.append(copies.send(nb.at[rows], rn.at[rows], other))
    dn_moves = {
        d: copies.send(down_sum.at[step(me, "y", d)], dn_in.at[d // 2], ys[d]) for d in (1, 3)
    }
    kept_back.append(moves.start(down_sum.at[step(me, "y", 2)], far_hbm))
    for zi in range(4):
        columns = og_all[:, :, :, pl.ds(384 * zi, 384)].reshape(GROUP * TOK, 384)
        sums = whole_tiles(tn(columns, hidden[...].reshape(all_units)).astype(bf16))
        down_terms[zi] = sums.reshape(4, 2, 48, COLUMNS)
    kept_back.append(moves.start(down_terms, down_hbm))
    aa_rows.complete(1, 3, 2)
    for copy in swaps_back:
        copy.wait_recv()
    grad_act = nb[...].astype(f32) + rn[...].astype(f32)
    inverse = inverse_of(resid[...])
    normed = resid[...] * inverse
    gain_terms[...] = jnp.sum(grad_act * normed, axis=0, keepdims=True)
    grad_normed = grad_act * gain
    inner = jnp.mean(grad_normed * normed, axis=-1, keepdims=True)
    grad_resid[...] = og[...].astype(f32) + inverse * (grad_normed - normed * inner)
    load_out.wait()
    grads[...] = nt(grad_resid[...].astype(bf16), w_out[...]).astype(bf16)
    for vmem, hbm in ((grad_resid, back_hbm), (grads, grads_hbm), (gain_terms, gains_hbm)):
        kept_back.append(moves.start(vmem, hbm))
    for d in (1, 3, 2):
        gate_moves[d].wait_recv()
    gate_sum[...] = whole_tiles((gate_terms[:, z_cols(0)].astype(f32) + three(gate_in)).T.astype(bf16))
    kept_back.append(moves.start(gate_sum, gate_sum_hbm))
    total = down_sum[y].astype(f32)
    for d in (1, 3):
        dn_moves[d].wait_recv()
        total = total + dn_in[d // 2].astype(f32)
    down_near[...] = total
    kept_back.append(moves.start(down_near, near_hbm))
    aa_rows.wait()
    moves.finish(kept_back)
    copies.finish()


def feed_forward(*arrays):
    rows = pltpu.VMEM((TOK, D), bf16)
    return pl.pallas_call(
        mlp_kernel,
        out_shape=[
            jax.ShapeDtypeStruct((TOK, D), f32),
            jax.ShapeDtypeStruct((TOK, HEADS * HD), bf16),
            jax.ShapeDtypeStruct((1, D), f32),
            jax.ShapeDtypeStruct((D // 4, COLUMNS), bf16),
            jax.ShapeDtypeStruct((TOK, D), f32),
            jax.ShapeDtypeStruct((TOK, D), bf16),
            jax.ShapeDtypeStruct((UNITS, D), bf16),
            jax.ShapeDtypeStruct((4, 4, 2, 48, COLUMNS), bf16),
            jax.ShapeDtypeStruct((4, 2, TOK, D), bf16),
        ],
        in_specs=[VMEM] * 4 + [ANY] * 5,
        out_specs=[ANY] * 9,
        scratch_shapes=[
            pltpu.VMEM((UNITS, D), bf16),
            pltpu.VMEM((4, 2, TOK, D), bf16),
            pltpu.VMEM((4, 2, TOK, D), bf16),
            pltpu.VMEM((4, 2 * TOK, UNITS), f32),
            *[pltpu.VMEM((4, 2 * TOK, UNITS), bf16)] * 3,
            *[pltpu.VMEM((4, 2, TOK, D), bf16)] * 2,
            *[pltpu.VMEM((4, TOK, D), bf16)] * 3,
            pltpu.VMEM((3, TOK, D), bf16),
            rows,
            rows,
            pltpu.VMEM((UNITS, D), bf16),
            pltpu.VMEM((3, UNITS, D // 4), bf16),
            *[pltpu.VMEM((D, COLUMNS), bf16)] * 2,
            pltpu.VMEM((UNITS, D), bf16),
            pltpu.VMEM((4, 4, 2, 48, COLUMNS), bf16),
            pltpu.VMEM((4, TOK, D), bf16),
            pltpu.VMEM((2, TOK, D), bf16),
            pltpu.VMEM((HEADS * HD, D), bf16),
            pltpu.VMEM((TOK, D), f32),
            pltpu.VMEM((TOK, HEADS * HD), bf16),
            pltpu.VMEM((1, D), f32),
            pltpu.VMEM((D // 4, COLUMNS), bf16),
            pltpu.VMEM((TOK, D), f32),
            *sems(48),
            pltpu.SemaphoreType.DMA((14,)),
        ],
        compiler_params=params(2),
    )(*arrays)


def back_kernel(*refs):
    lengths, lse, grad_resid, grads_in, gain, mlp_gain_terms = refs[:6]
    x_hbm, rope_hbm, gate_sum, down_far, q_hbm, kv_hbm, exact_hbm, resid_hbm, near_hbm = refs[6:15]
    al_hbm, w_qkv_hbm, act_hbm, up_terms, wd_terms = refs[15:20]
    results_hbm = refs[20:28]
    (g, stats, acc, acc_in, dkv, r1a, r1b, ta, tb, r2a, r2b, u, r3, w_qkv, act_all, gbt, gbt_all, al_all) = refs[28:46]
    gp, gp_flat, gp_all, part, part_other, small, e1, e2, e3, f1, f2 = refs[46:57]
    up_own, up_in, up_mid, wd_own, wd_across, wd_sum, wd_in, wd_mid, wd_second = refs[57:66]
    gate_second, up_second = refs[66:68]
    summed, third_in = refs[68:71], refs[71:74]
    q_terms, q_first, q_mid, q_second, q_summed, q_third = refs[74:80]
    down_in, down_part, down_other, q, kv, exact, resid, down_near, o_half, o_core, o_sum, o_in, o_mid, o_across, o_fin, o_third, *refs = refs[80:]
    x, rope, in_grad, layer_out, sum_gate, sum_up, sum_down, sum_qkv, sum_out, small_out, *refs = refs
    send_sems, recv_sems, local_sems = refs

    me = here()
    ids, start = token_rows(me, lengths)
    z, y, xh, c, n = (me[a] for a in AXES)
    partner, across, other = at(me, c=1), at(me, xh=1), at(me, n=1)
    ys = {d: at(me, y=d) for d in (1, 2, 3)}
    zs = {d: at(me, z=d) for d in (1, 2, 3)}
    near_moves = [(d, e) for d in (1, 3, 2, 0) for e in (0, 1) if d or e]
    near = {m: at(me, y=m[0], xh=m[1]) for m in near_moves}
    group = {m: at(me, y=m[0], c=m[1]) for m in near_moves}
    def strip(yi, xi):
        return pl.ds(pl.multiple_of(96 * yi + 48 * xi, 48), 48)

    everyone_in = hail([other, *zs.values(), *near.values(), *(group[m] for m in near_moves if m[1])])
    moves, kept_back = Moves(local_sems), []
    load = moves.start

    def keep_result(k, vmem):
        kept_back.append(moves.start(vmem, results_hbm[k]))

    loads = [load(exact_hbm, exact), load(q_hbm, q), load(kv_hbm, kv)]
    load_resid, load_near = load(resid_hbm, resid), load(near_hbm, down_near)
    load_x, load_rope = load(x_hbm, x), load(rope_hbm, rope)
    load_strip = load(gate_sum.at[strip(y, xh)], gate_second.at[y, xh])
    half = TOK // 2
    low, high = pl.ds(0, half), pl.ds(half, half)
    gbt[...] = grad_resid[...].T.astype(bf16).reshape(4, 4, 96, TOK)
    for h in range(HEADS):
        g[c, pl.ds(h * TOK, TOK), :] = grads_in[:, h * HD : (h + 1) * HD]
    loads[0].wait()
    stats[c, 0:1, :] = lse[...]
    stats[c, 1:2, :] = jnp.sum(g[c].astype(f32).T * exact[...], axis=0, keepdims=True)
    stats[c, 2:8, :] = jnp.zeros((6, NQ), f32)
    everyone_in()
    copies = Copies(send_sems, recv_sems)
    shared = [copies.send(g.at[c], g.at[c], partner), copies.send(stats.at[c], stats.at[c], partner)]

    def z_cols(d):
        return pl.ds(pl.multiple_of(step(me, "z", d) * 384, 384), 384)

    second = {}

    def send_second(i, source, in_ref):
        for m in near_moves:
            second[i, m] = copies.send(
                source(step(me, "y", m[0]), step(me, "xh", m[1])), in_ref.at[y, xh], near[m]
            )

    def send_mid(i, total, mid_ref, in_ref):
        turned = total.T.astype(bf16)
        if turned.shape[1] == UNITS:
            turned = whole_tiles(turned)
        for yi in range(4):
            for xi in range(2):
                rows = 96 * yi + 48 * xi
                mid_ref[yi, xi] = turned[rows : rows + 48]
        send_second(i, lambda yi, xi: mid_ref.at[yi, xi], in_ref)
        in_ref[y, xh] = mid_ref[y, xh]

    keep, give = pl.ds(pl.multiple_of(24 * c, 8), 24), pl.ds(pl.multiple_of(24 * (1 - c), 8), 24)
    third = {}
    all_summed = [*summed, q_summed]
    all_second = [gate_second, up_second, None, q_second]
    all_third = [*third_in, q_third]
    outs = (sum_gate, sum_up, sum_down, sum_qkv)

    def collect(i):
        if i == 2:
            for d in (1, 3, 2):
                second[2, d].wait_recv()
            summed[2][...] = wd_second[...].astype(f32)
        else:
            for m in near_moves:
                second[i, m].wait_recv()
            all_summed[i][...] = all_second[i][:, 0].astype(f32) + all_second[i][:, 1].astype(f32)
        third[i] = copies.send(all_summed[i].at[:, give], all_third[i], partner)

    def deliver(i):
        third[i].wait_recv()
        for yi in range(4):
            mine_sum, their_sum = all_summed[i][yi, keep], all_third[i][yi]
            pair = (jnp.where(c == 0, mine_sum, their_sum), jnp.where(c == 0, their_sum, mine_sum))
            for e in range(2):
                k = 2 * yi + e
                width = UNITS if i < 3 else HD
                outs[i][:, pl.ds(k * width, width)] = pair[e][:, :width]

    send_second(0, lambda yi, xi: gate_sum.at[strip(yi, xi)], gate_second)
    gbt_moves = {
        d: copies.send(gbt.at[:, step(me, "y", d)], gbt_all.at[y], ys[d]) for d in (1, 3, 2)
    }
    gbt_all[y] = gbt[:, y]
    down_move = copies.send(down_far, down_in, ys[2])
    first = {}
    for d in (1, 3, 2):
        first[d] = copies.send(up_terms.at[:, z_cols(d)], up_in.at[d - 1], zs[d])
    wd_move = copies.send(wd_terms.at[:, :, 1 - xh], wd_across, across)

    load_al = load(al_hbm, al_all)
    load_w = load(w_qkv_hbm, w_qkv)
    load_act = load(act_hbm, act_all)
    load_up = load(up_terms.at[:, z_cols(0)], up_own)
    load_wd = load(wd_terms.at[:, :, xh], wd_own)

    for copy in shared:
        copy.wait_recv()
    for copy in loads[1:]:
        copy.wait()
    acc[...] = jnp.zeros_like(acc)
    last = shard_of(me) // BLOCK_SHARDS

    def of_both(row):
        return jnp.concatenate([stats[0, row : row + 1, :], stats[1, row : row + 1, :]], axis=1)

    log_total, balance = of_both(0), of_both(1)
    earlier = jnp.where(start < last * KEY_BLOCK, log_total, -big_negative)
    keys_here = 2 * TOK

    def block(index, masked, shift):
        zi, yi = index // 4, lax.rem(index, 4)
        keys = kv[zi, yi, :, :, pl.ds(0, HD)].reshape(keys_here, HD)
        values = kv[zi, yi, :, :, pl.ds(HD, HD)].reshape(keys_here, HD)
        keys_t = keys.T
        dk = jnp.zeros((keys_here, HD), f32)
        dv = jnp.zeros((keys_here, HD), f32)
        for chunk in range(2 * NQ // Q_CHUNK):
            core, cs = divmod(chunk * Q_CHUNK, NQ)
            cs = pl.ds(cs, Q_CHUNK)
            piece = slice(chunk * Q_CHUNK, (chunk + 1) * Q_CHUNK)
            qc, gc = q[core, cs, :], g[core, cs, :]
            probs = jnp.exp2(nt(keys, qc) * SCALE_LOG2 - shift[:, piece])
            if masked:
                place = lax.broadcasted_iota(jnp.int32, (keys_here, Q_CHUNK), 0)
                key_ids = index * KEY_BLOCK + c * TOK + place + place // TOK * TOK
                allowed = (key_ids >= start[:, piece]) & (key_ids <= ids[:, piece])
                probs = jnp.where(allowed, probs, 0.0)
            grads = (probs * (nt(values, gc) - balance[:, piece])).astype(bf16)
            dv = dv + nn(probs.astype(bf16), gc)
            dk = dk + nn(grads, qc)
            acc[core, :, cs] = acc[core, :, cs] + nn(keys_t, grads)
        dkv[zi, yi, :, :, pl.ds(0, HD)] = (dk * SCALE).astype(bf16).reshape(2, TOK, HD)
        dkv[zi, yi, :, :, pl.ds(HD, HD)] = dv.astype(bf16).reshape(2, TOK, HD)

    def segment(zi):
        @pl.loop(0, 4)
        def _(yi):
            index = 4 * zi + yi
            edge = (index == 0) | (index == last)

            @pl.when(edge & (index <= last))
            def _():
                block(index, True, jnp.where(index == last, log_total, earlier))

            @pl.when((index < last) & jnp.logical_not(edge))
            def _():
                block(index, False, earlier)

            @pl.when(index > last)
            def _():
                dkv[zi, yi] = jnp.zeros((2, TOK, 2 * HD), bf16)

    first_a, first_b, second_a, second_b = {}, {}, {}, {}

    def settle(d):
        zi = step(me, "z", d)
        if d:
            first_a[d] = copies.send(dkv.at[zi, :, :, low], r1a.at[d - 1], zs[d])
        for e in (1, 3, 2):
            first_b[d, e] = copies.send(
                dkv.at[zi, step(me, "y", e), :, high], r1b.at[e - 1, zi], ys[e]
            )

    segment(step(me, "z", 1))
    settle(1)
    segment(step(me, "z", 2))
    settle(2)
    segment(step(me, "z", 3))
    settle(3)
    load_al.wait()
    for d in (1, 3, 2):
        gbt_moves[d].wait_recv()
    every_al = al_all[...].reshape(4 * TOK, HEADS * HD)
    for zi in range(4):
        lhs = jnp.concatenate([gbt_all[yi, zi] for yi in range(4)], axis=1)
        terms = nn(lhs, every_al).astype(bf16)
        o_half[0, zi] = terms[:, : HEADS * HD // 2]
        o_half[1, zi] = terms[:, HEADS * HD // 2 :]
    o_move = copies.send(o_half.at[1 - c], o_core, partner)
    segment(z)
    settle(0)
    queries_back = copies.send(acc.at[1 - c], acc_in, partner)
    down_move.wait_recv()
    load_near.wait()
    down_part[...] = (down_near[...] + down_in[...].astype(f32)).astype(bf16)
    down_swap = copies.send(down_part, down_other, other)
    for d in (1, 3, 2):
        first_a[d].wait_recv()
    ta[...] = (dkv[z, :, :, low].astype(f32) + three(r1a)).astype(bf16)
    for d in (1, 3, 2):
        second_a[d] = copies.send(ta.at[step(me, "y", d)], r2a.at[d - 1], ys[d])
    for copy in first_b.values():
        copy.wait_recv()
    tb[...] = (dkv[:, y, :, high].astype(f32) + three(r1b)).astype(bf16)
    for d in (1, 3, 2):
        second_b[d] = copies.send(tb.at[step(me, "z", d)], r2b.at[d - 1], zs[d])
    for d in (1, 3, 2):
        second_a[d].wait_recv()
        second_b[d].wait_recv()
    ua = ta[y].astype(f32) + three(r2a)
    ub = tb[z].astype(f32) + three(r2b)
    u[:, low] = ua.astype(bf16)
    u[:, high] = ub.astype(bf16)
    kv_last = copies.send(u.at[1 - xh], r3, across)
    load_wd.wait()
    wd_move.wait_recv()
    for zi in range(4):
        wd_sum[zi] = (wd_own[zi].astype(f32) + wd_across[zi].astype(f32)).astype(bf16)
    wd_first = {d: copies.send(wd_sum.at[step(me, "z", d)], wd_in.at[d - 1], zs[d]) for d in (1, 3, 2)}
    o_move.wait_recv()
    o_sum[...] = (o_half[c].astype(f32) + o_core[...].astype(f32)).astype(bf16)
    o_first = {d: copies.send(o_sum.at[step(me, "z", d)], o_in.at[d - 1], zs[d]) for d in (1, 3, 2)}
    queries_back.wait_recv()
    load_rope.wait()
    load_x.wait()
    turned_back = ((acc[c] + acc_in[...]) * SCALE).T

    def revert(rows):
        return rows * rope[0] - pltpu.roll(rows, HD // 2, 1) * rope[1]

    def keep_head(h, rows):
        low_rows = rows.astype(bf16)
        gp[h] = low_rows
        gp_flat[:, pl.ds(h * HD, HD)] = low_rows
        small[pl.ds(24 + h, 1), :] = jnp.sum(low_rows.astype(f32), axis=0, keepdims=True)

    def to_small(first_row, row):
        for k in range(D // 128):
            small[pl.ds(first_row + k, 1), :] = row[:, k * 128 : (k + 1) * 128]

    small[...] = jnp.zeros_like(small)
    to_small(12, mlp_gain_terms[...])
    for h in range(HEADS):
        keep_head(h, revert(turned_back[h * TOK : (h + 1) * TOK]))
    load_w.wait()
    front = HEADS * HD
    partial = nt(gp_flat[:, pl.ds(0, front)], w_qkv[:, pl.ds(0, front)])

    kv_last.wait_recv()
    grad_kv = u[xh].astype(f32) + r3[...].astype(f32)
    keep_head(HEADS, revert(grad_kv[:, :HD]))
    keep_head(HEADS + 1, grad_kv[:, HD:])
    gp_moves = [
        copies.send(gp.at[step(me, "y", m[0]) * 2 + step(me, "c", m[1])], gp_all.at[y, c], group[m])
        for m in near_moves
    ]
    gp_all[y, c] = gp[y * 2 + c]
    back = pl.ds(front, 2 * HD)
    part[...] = (partial + nt(gp_flat[:, back], w_qkv[:, back])).astype(bf16)
    swap = copies.send(part, part_other, other)
    load_up.wait()
    for d in (1, 3, 2):
        first[d].wait_recv()
    send_mid(1, up_own[...].astype(f32) + three(up_in), up_mid, up_second)
    load_strip.wait()
    collect(0)
    load_act.wait()
    for copy in gp_moves:
        copy.wait_recv()
    q_terms[...] = tn(
        gp_all[...].reshape(GROUP * TOK, HD), act_all[...].reshape(GROUP * TOK, D)
    ).astype(bf16)

    q_one = {d: copies.send(q_terms.at[:, z_cols(d)], q_first.at[d - 1], zs[d]) for d in (1, 3, 2)}
    down_swap.wait_recv()
    load_resid.wait()
    layer_out[...] = (
        resid[...] + (down_part[...].astype(f32) + down_other[...].astype(f32))
    ).astype(bf16)
    keep_result(1, layer_out)
    swap.wait_recv()
    grad_act = part[...].astype(f32) + part_other[...].astype(f32)
    rows = x[...].astype(f32)
    inverse = lax.rsqrt(jnp.mean(rows * rows, axis=-1, keepdims=True) + rms_eps)
    normed = rows * inverse
    to_small(0, jnp.sum(grad_act * normed, axis=0, keepdims=True))
    small_one = {d: copies.send(small, e1.at[d - 1], zs[d]) for d in (1, 3, 2)}
    grad_normed = grad_act * gain[...].reshape(1, D)
    inner = jnp.mean(grad_normed * normed, axis=-1, keepdims=True)
    in_grad[...] = (grad_resid[...] + inverse * (grad_normed - normed * inner)).astype(bf16)

    keep_result(0, in_grad)
    for d in (1, 3, 2):
        wd_first[d].wait_recv()
    wd_mid[...] = (wd_sum[z].astype(f32) + three(wd_in)).astype(bf16)
    for d in (1, 3, 2):
        second[2, d] = copies.send(wd_mid.at[step(me, "y", d)], wd_second.at[y], ys[d])
    wd_second[y] = wd_mid[y]
    for d in (1, 3, 2):
        o_first[d].wait_recv()
    o_total = (o_sum[z].astype(f32) + three(o_in)).astype(bf16)
    o_mid[0], o_mid[1] = o_total[:48], o_total[48:]
    o_last = copies.send(o_mid.at[1 - xh], o_across, across)
    for d in (1, 3, 2):
        q_one[d].wait_recv()
    send_mid(3, q_terms[:, z_cols(0)].astype(f32) + three(q_first), q_mid, q_second)
    for d in (1, 3, 2):
        small_one[d].wait_recv()
    f1[...] = small[...] + three(e1)
    small_two = {m: copies.send(f1, e2.at[k], near[m]) for k, m in enumerate(near_moves)}
    o_last.wait_recv()
    o_fin[...] = o_mid[xh].astype(f32) + o_across[...].astype(f32)
    o_end = copies.send(o_fin.at[give], o_third, partner)
    collect(1)
    deliver(0)
    keep_result(2, sum_gate)
    deliver(1)
    keep_result(3, sum_up)
    collect(2)
    collect(3)
    for m in near_moves:
        small_two[m].wait_recv()
    f2[...] = f1[...]
    for k in range(len(near_moves)):
        f2[...] = f2[...] + e2[k]
    small_three = copies.send(f2, e3, partner)
    deliver(2)
    keep_result(4, sum_down)
    deliver(3)
    keep_result(5, sum_qkv)
    o_end.wait_recv()
    o_mine, o_theirs = o_fin[keep], o_third[...]
    sum_out[:, : HEADS * HD // 2] = jnp.where(c == 0, o_mine, o_theirs)
    sum_out[:, HEADS * HD // 2 :] = jnp.where(c == 0, o_theirs, o_mine)
    keep_result(6, sum_out)
    small_three.wait_recv()
    small_out[...] = f2[...] + e3[...]
    keep_result(7, small_out)
    moves.finish(kept_back)
    copies.finish()


def back(*arrays):
    half = TOK // 2
    wide = 2 * HD
    results_of = [
        jax.ShapeDtypeStruct((TOK, D), bf16),
        jax.ShapeDtypeStruct((TOK, D), bf16),
        *[jax.ShapeDtypeStruct((24, FF // 2), f32)] * 3,
        jax.ShapeDtypeStruct((24, (HEADS + 2) * HD), f32),
        jax.ShapeDtypeStruct((24, HEADS * HD), f32),
        jax.ShapeDtypeStruct((40, 128), f32),
    ]
    return pl.pallas_call(
        back_kernel,
        out_shape=results_of,
        in_specs=[SMEM] + [VMEM] * 5 + [ANY] * 14,
        out_specs=[ANY] * 8,
        scratch_shapes=[
            pltpu.VMEM((2, NQ, HD), bf16),
            pltpu.VMEM((2, 8, NQ), f32),
            pltpu.VMEM((2, HD, NQ), f32),
            pltpu.VMEM((HD, NQ), f32),
            pltpu.VMEM((4, 4, 2, TOK, wide), bf16),
            pltpu.VMEM((3, 4, 2, half, wide), bf16),
            pltpu.VMEM((3, 4, 2, half, wide), bf16),
            pltpu.VMEM((4, 2, half, wide), bf16),
            pltpu.VMEM((4, 2, half, wide), bf16),
            pltpu.VMEM((3, 2, half, wide), bf16),
            pltpu.VMEM((3, 2, half, wide), bf16),
            pltpu.VMEM((2, TOK, wide), bf16),
            pltpu.VMEM((TOK, wide), bf16),
            pltpu.VMEM((D, (HEADS + 2) * HD), bf16),
            pltpu.VMEM((4, 2, TOK, D), bf16),
            pltpu.VMEM((4, 4, 96, TOK), bf16),
            pltpu.VMEM((4, 4, 96, TOK), bf16),
            pltpu.VMEM((4, TOK, HEADS * HD), bf16),
            pltpu.VMEM((HEADS + 2, TOK, HD), bf16),
            pltpu.VMEM((TOK, (HEADS + 2) * HD), bf16),
            pltpu.VMEM((4, 2, TOK, HD), bf16),
            pltpu.VMEM((TOK, D), bf16),
            pltpu.VMEM((TOK, D), bf16),
            pltpu.VMEM((40, 128), f32),
            pltpu.VMEM((3, 40, 128), f32),
            pltpu.VMEM((7, 40, 128), f32),
            pltpu.VMEM((40, 128), f32),
            pltpu.VMEM((40, 128), f32),
            pltpu.VMEM((40, 128), f32),
            pltpu.VMEM((UNITS, 384), bf16),
            pltpu.VMEM((3, UNITS, 384), bf16),
            pltpu.VMEM((4, 2, 48, COLUMNS), bf16),
            *[pltpu.VMEM((4, 4, 48, COLUMNS), bf16)] * 3,
            pltpu.VMEM((3, 4, 48, COLUMNS), bf16),
            *[pltpu.VMEM((4, 48, COLUMNS), bf16)] * 2,
            *[pltpu.VMEM((4, 2, 48, COLUMNS), bf16)] * 2,
            *[pltpu.VMEM((4, 48, COLUMNS), f32)] * 3,
            *[pltpu.VMEM((4, 24, COLUMNS), f32)] * 3,
            pltpu.VMEM((HD, D), bf16),
            pltpu.VMEM((3, HD, 384), bf16),
            pltpu.VMEM((4, 2, 48, HD), bf16),
            pltpu.VMEM((4, 2, 48, HD), bf16),
            pltpu.VMEM((4, 48, HD), f32),
            pltpu.VMEM((4, 24, HD), f32),
            pltpu.VMEM((TOK, D), bf16),
            pltpu.VMEM((TOK, D), bf16),
            pltpu.VMEM((TOK, D), bf16),
            pltpu.VMEM((2, NQ, HD), bf16),
            pltpu.VMEM((4, 4, 2, TOK, wide), bf16),
            pltpu.VMEM((HD, NQ), f32),
            pltpu.VMEM((TOK, D), f32),
            pltpu.VMEM((TOK, D), f32),
            pltpu.VMEM((2, 4, 96, HEADS * HD // 2), bf16),
            *[pltpu.VMEM((4, 96, HEADS * HD // 2), bf16)] * 2,
            pltpu.VMEM((3, 96, HEADS * HD // 2), bf16),
            pltpu.VMEM((2, 48, HEADS * HD // 2), bf16),
            pltpu.VMEM((48, HEADS * HD // 2), bf16),
            pltpu.VMEM((48, HEADS * HD // 2), f32),
            pltpu.VMEM((24, HEADS * HD // 2), f32),
            pltpu.VMEM((TOK, D), bf16),
            pltpu.VMEM((2, TOK, HD), f32),
            *[pltpu.VMEM(a.shape, a.dtype) for a in results_of],
            *sems(93),
            pltpu.SemaphoreType.DMA((21,)),
        ],
        compiler_params=params(9, 62),
    )(*arrays)


def results_kernel(*refs):
    wholes, small, copied = refs[:7], refs[7], refs[8:15]
    norm_attn, norm_mlp, bias, value_bias, *held, into, out_of = refs[15:]
    shard = shard_of(here())
    loads, stores = Moves(into), Moves(out_of)
    for a, b in zip(wholes, held):
        loads.start(a, b)
    rows = jnp.concatenate(
        [
            jnp.concatenate([small[12 * i + k : 12 * i + k + 1, :] for k in range(12)], axis=1)
            for i in range(2)
        ],
        axis=0,
    )
    turned = pltpu.roll(rows, lax.rem(D - 24 * shard, D), 1)
    norm_attn[...] = turned[0:1, :24]
    norm_mlp[...] = turned[1:2, :24]
    heads = pltpu.roll(small[24 : 24 + HEADS + 2, :], lax.rem(HD - 2 * shard, HD), 1)
    bias[0] = heads[: HEADS + 1, :2].T
    value_bias[...] = heads[HEADS + 1 :, :2]
    for load, a, b in zip(loads.started, held, copied):
        load.wait()
        stores.start(a, b)
    stores.finish(stores.started)


def results(*arrays):
    *wholes, small = arrays
    return pl.pallas_call(
        results_kernel,
        out_shape=[
            *[jax.ShapeDtypeStruct(a.shape, a.dtype) for a in wholes],
            jax.ShapeDtypeStruct((1, 24), f32),
            jax.ShapeDtypeStruct((1, 24), f32),
            jax.ShapeDtypeStruct((1, 2, HEADS + 1), f32),
            jax.ShapeDtypeStruct((1, 2), f32),
        ],
        in_specs=[ANY] * 7 + [VMEM],
        out_specs=[ANY] * 7 + [VMEM] * 4,
        scratch_shapes=[
            *[pltpu.VMEM(a.shape, a.dtype) for a in wholes],
            *[pltpu.SemaphoreType.DMA((7,))] * 2,
        ],
    )(*wholes, small)


def shards(
    layer_in, lengths, norm_attn, w_qkv, qkv_bias, w_out, norm_mlp, w_gate, w_up, w_down, out_grad
):
    half = HD // 2
    freqs = np.float32(rope_base) ** (-2.0 * np.arange(half, dtype=np.float32) / HD)
    freqs = np.concatenate([freqs, freqs]).astype(np.float32)[None]
    kv, queries, act_attn, resid, exact, lse, rope, gate_w, up_w, out_grad_all, low_all = attend(
        lengths, layer_in, norm_attn, qkv_bias, freqs, out_grad, w_qkv, w_out, w_gate, w_up
    )
    (
        grad_resid, grads, gain_terms, gate_sum, down_near, down_far,
        up_terms, down_terms, act_attn_all,
    ) = feed_forward(
        resid, norm_mlp, out_grad, act_attn, w_out, out_grad_all, gate_w, up_w, w_down
    )
    sums = back(
        lengths, lse, grad_resid, grads, norm_attn, gain_terms, layer_in, rope, gate_sum, down_far,
        queries, kv, exact, resid, down_near, low_all, w_qkv, act_attn_all, up_terms, down_terms,
    )
    in_grad, layer_out, sum_gate, sum_up, sum_down, sum_qkv, sum_out, *rest = results(*sums)
    sum_norm_attn, sum_norm_mlp, bias, value_bias = rest
    return (
        layer_out,
        in_grad,
        sum_norm_attn[0],
        sum_qkv,
        bias.swapaxes(1, 2),
        value_bias,
        sum_out.T,
        sum_norm_mlp[0],
        sum_gate,
        sum_up,
        sum_down.T,
    )


def solution(mesh):
    torus = Mesh(mesh.devices.reshape(4, 4, 2, 2, 2), AXES)
    in_specs = (
        P(WIDE, None),
        P(),
        P(),
        P(None, "n"),
        P("n", None),
        P("n", None),
        P(),
        P(None, "n"),
        P(None, "n"),
        P("n", None),
        P(WIDE, None),
    )
    out_specs = (
        P(WIDE, None),
        P(WIDE, None),
        P(WIDE),
        P(WIDE, "n"),
        P("n", None, WIDE),
        P("n", WIDE),
        P("n", WIDE),
        P(WIDE),
        P(WIDE, "n"),
        P(WIDE, "n"),
        P("n", WIDE),
    )
    return jax.shard_map(
        shards, mesh=torus, in_specs=in_specs, out_specs=out_specs, check_vma=False
    )
```

profile of v0, /device:TPU:1, one launch (start us, length us, event | category | flops | bytes accessed | tf_op | source)
XLA Modules:
  0.0 193.1 jit_solution(9911209830960422060)
XLA Ops:
  0.6 46.7 %shard_map.203 = (bf16[4,4,2,128,256]{4,3,2,1,0:T(8,128)(2,1)}, bf16[2,768,128]{2,1,0:T(8,128)(2,1)}, bf16[128,1536]{1,0:T(8,128)(2,1)}, f32[128,1536]{1,0:T(8,1...) custom-call(s32[4]{0:T(128)} %refs_0_.1, ...), custom_call_target="tpu_custom_call" | custom-call | tf_op jit(solution)/shard_map/pallas_call | solution.py:454
  47.4 67.1 %shard_map.204 = (f32[128,1536]{1,0:T(8,128)}, bf16[128,768]{1,0:T(8,128)(2,1)}, f32[1,1536]{1,0:T(1,128)}, bf16[384,640]{1,0:T(8,128)(2,1)}, f32[128,1536]{1,0:...) custom-call(f32[128,1536]{1,0:T(8,128)} %get-tuple-element.51.refs_0, ...), custom_call_target="tpu_custom_call" | custom-call | tf_op jit(solution)/shard_map/pallas_call | solution.py:667
  114.5 74.6 %shard_map.205 = (bf16[128,1536]{1,0:T(8,128)(2,1)}, bf16[128,1536]{1,0:T(8,128)(2,1)}, f32[24,4480]{1,0:T(8,128)}, f32[24,4480]{1,0:T(8,128)}, f32[24,4480]{1,0...) custom-call(s32[4]{0:T(128)} %refs_0_.1, f32[1,768]{1,0:T(1,128)} %get-tuple-element.50.refs_1_, ...), custom_call_target="tpu_custom_call" | custom-call | tf_op jit(solution)/shard_map/pallas_call | solution.py:1079
  189.1 3.8 %shard_map.206 = (bf16[128,1536]{1,0:T(8,128)(2,1)}, bf16[128,1536]{1,0:T(8,128)(2,1)}, f32[24,4480]{1,0:T(8,128)}, f32[24,4480]{1,0:T(8,128)}, f32[24,4480]{1,0...) custom-call(bf16[128,1536]{1,0:T(8,128)(2,1)} %get-tuple-element.70., ...), custom_call_target="tpu_custom_call" | custom-call | tf_op jit(solution)/shard_map/pallas_call | solution.py:1182
where the time goes:
time: 197 us; the launch traced here: 193 us
  Pallas kernels  192 us (97%)
    pallas_call x1, Pallas kernels, back(): pl.pallas_call(back_kernel, out_shape=results_of, in_specs=[SMEM] + [VMEM...  74.6 us
    pallas_call x1, Pallas kernels, feed_forward(): pl.pallas_call(mlp_kernel, out_shape=[jax.ShapeDtypeStruct((TOK, D), f32)...  67.1 us
    pallas_call x1, Pallas kernels, attend(): pl.pallas_call(attend_kernel, out_shape=[*state, jax.ShapeDtypeStruct((4,...  46.7 us

commit v1 on v0

--- a/solution.py
+++ b/solution.py
@@ -261,7 +261,9 @@
     half = TOK // 2
     keys_here = 2 * half
 
-    def take(parts, masked):
+    early = sequence_starts(last * KEY_BLOCK - 1, lengths)
+
+    def take(parts, masked=False, from_first=False):
         def both(columns):
             return jnp.concatenate(
                 [
@@ -273,19 +275,27 @@
                 axis=0,
             )
 
+        def key_ids(columns):
+            place = lax.broadcasted_iota(jnp.int32, (keys_here, columns), 0)
+            place = place + place // half * (2 * TOK - half)
+            return jnp.concatenate(
+                [(4 * zi + yi) * KEY_BLOCK + c * TOK + half * k + place for zi, yi, k in parts], axis=0
+            )
+
         keys, values = both(pl.ds(0, HD)), both(pl.ds(HD, HD)).T
+        if from_first:
+            barred = jnp.where(key_ids(1) >= early, 0.0, big_negative)
         for chunk in range(2 * NQ // Q_CHUNK):
             core, cs = divmod(chunk * Q_CHUNK, NQ)
             cs = pl.ds(cs, Q_CHUNK)
             here_cols = slice(chunk * Q_CHUNK, (chunk + 1) * Q_CHUNK)
             scores = nt(keys, q[core, cs, :]) * SCALE_LOG2
             if masked:
-                ((zi, yi, k),) = parts
-                place = lax.broadcasted_iota(jnp.int32, (keys_here, Q_CHUNK), 0)
-                first_key = (4 * zi + yi) * KEY_BLOCK + c * TOK + half * k
-                key_ids = first_key + place + place // half * (2 * TOK - half)
-                allowed = (key_ids >= start[:, here_cols]) & (key_ids <= ids[:, here_cols])
+                which = key_ids(Q_CHUNK)
+                allowed = (which >= start[:, here_cols]) & (which <= ids[:, here_cols])
                 scores = jnp.where(allowed, scores, big_negative)
+            if from_first:
+                scores = scores + barred
             old = stats[core, 0:1, cs]
             new = jnp.maximum(old, jnp.max(scores, axis=0, keepdims=True))
             if masked:
@@ -304,13 +314,19 @@
 
     def pair(za, ya, zb, yb):
         a, b = 4 * za + ya, 4 * zb + yb
-        inner = (jnp.minimum(a, b) > 0) & (jnp.maximum(a, b) < last)
-
-        @pl.when(inner)
+        spots = [(za, ya, 0), (zb, yb, 1)]
+        before_last = jnp.maximum(a, b) < last
+        has_first = jnp.minimum(a, b) == 0
+
+        @pl.when(before_last & jnp.logical_not(has_first))
         def _():
-            take([(za, ya, 0), (zb, yb, 1)], False)
-
-        @pl.when(jnp.logical_not(inner))
+            take(spots)
+
+        @pl.when(before_last & has_first)
+        def _():
+            take(spots, from_first=True)
+
+        @pl.when(jnp.logical_not(before_last))
         def _():
             @pl.loop(0, 2)
             def _(k):
@@ -320,11 +336,30 @@
 
                 @pl.when(edge & (index <= last))
                 def _():
-                    take([(zi, yi, k)], True)
+                    take([(zi, yi, k)], masked=True)
 
                 @pl.when((index < last) & jnp.logical_not(edge))
                 def _():
-                    take([(zi, yi, k)], False)
+                    take([(zi, yi, k)])
+
+    def two_pairs(one, two):
+        spots = [(*one[:2], 0), (*one[2:], 1), (*two[:2], 0), (*two[2:], 1)]
+        index = [4 * zi + yi for zi, yi, _ in spots]
+        least = jnp.minimum(jnp.minimum(index[0], index[1]), jnp.minimum(index[2], index[3]))
+        most = jnp.maximum(jnp.maximum(index[0], index[1]), jnp.maximum(index[2], index[3]))
+        @pl.when((most < last) & (least > 0))
+        def _():
+            take(spots)
+
+        @pl.when((most < last) & (least == 0))
+        def _():
+            take(spots, from_first=True)
+
+        @pl.when(most >= last)
+        def _():
+            @pl.loop(0, 2)
+            def _(i):
+                pair(*(jnp.where(i == 0, a, b) for a, b in zip(one, two)))
 
     first.wait_recv()
     low, high = pl.ds(0, half), pl.ds(half, half)
@@ -347,7 +382,7 @@
     window = pl.ds(pl.multiple_of(tile * 128, 128), WINDOW)
     load_gate = moves.start(w_gate_hbm.at[:, window], wide_gate)
     load_up = moves.start(w_up_hbm.at[:, window], wide_up)
-    pair(z, y, z, y)
+    take([(z, y, 0), (z, y, 1)], masked=True)
     second_from = copies.used
     copies.used += 24
     for i, e in enumerate((0, 1, 3, 2)):
@@ -381,11 +416,15 @@
         one, two = slot(za, ya, low), slot(zb, yb, high)
         copies.numbered(second_from + 2 * k, one, one, zs[1]).wait_recv()
         copies.numbered(second_from + 2 * k + 1, two, two, ys[1]).wait_recv()
-        pair(za, ya, zb, yb)
-
-    pl.loop(0, 8)(arrive)
+
+    def two_arrive(i):
+        arrive(2 * i)
+        arrive(2 * i + 1)
+        two_pairs(places(2 * i), places(2 * i + 1))
+
+    pl.loop(0, 4)(two_arrive)
     rows_of_og.pass_on(2)
-    pl.loop(8, 12)(arrive)
+    pl.loop(4, 6)(two_arrive)
     kept_back.append(moves.start(kv, kv_hbm))
     merge = [
         copies.send(stats.at[1 - c], stats_in, partner),
@@ -944,7 +983,6 @@
     wd_first = {d: copies.send(wd_sum.at[step(me, "z", d)], wd_in.at[d - 1], zs[d]) for d in (1, 3, 2)}
     o_move.wait_recv()
     o_sum[...] = (o_half[c].astype(f32) + o_core[...].astype(f32)).astype(bf16)
-    o_first = {d: copies.send(o_sum.at[step(me, "z", d)], o_in.at[d - 1], zs[d]) for d in (1, 3, 2)}
     queries_back.wait_recv()
     load_rope.wait()
     load_x.wait()
@@ -997,6 +1035,7 @@
     ).astype(bf16)
 
     q_one = {d: copies.send(q_terms.at[:, z_cols(d)], q_first.at[d - 1], zs[d]) for d in (1, 3, 2)}
+    o_first = {d: copies.send(o_sum.at[step(me, "z", d)], o_in.at[d - 1], zs[d]) for d in (1, 3, 2)}
     down_swap.wait_recv()
     load_resid.wait()
     layer_out[...] = (
@@ -1022,13 +1061,13 @@
         second[2, d] = copies.send(wd_mid.at[step(me, "y", d)], wd_second.at[y], ys[d])
     wd_second[y] = wd_mid[y]
     for d in (1, 3, 2):
+        q_one[d].wait_recv()
+    send_mid(3, q_terms[:, z_cols(0)].astype(f32) + three(q_first), q_mid, q_second)
+    for d in (1, 3, 2):
         o_first[d].wait_recv()
     o_total = (o_sum[z].astype(f32) + three(o_in)).astype(bf16)
     o_mid[0], o_mid[1] = o_total[:48], o_total[48:]
     o_last = copies.send(o_mid.at[1 - xh], o_across, across)
-    for d in (1, 3, 2):
-        q_one[d].wait_recv()
-    send_mid(3, q_terms[:, z_cols(0)].astype(f32) + three(q_first), q_mid, q_second)
     for d in (1, 3, 2):
         small_one[d].wait_recv()
     f1[...] = small[...] + three(e1)
@@ -1153,7 +1192,8 @@
 
 def results_kernel(*refs):
     wholes, small, copied = refs[:7], refs[7], refs[8:15]
-    norm_attn, norm_mlp, bias, value_bias, *held, into, out_of = refs[15:]
+    small_outs, (norm_attn, norm_mlp, bias, value_bias) = refs[15:19], refs[19:23]
+    *held, into, out_of = refs[23:]
     shard = shard_of(here())
     loads, stores = Moves(into), Moves(out_of)
     for a, b in zip(wholes, held):
@@ -1171,6 +1211,8 @@
     heads = pltpu.roll(small[24 : 24 + HEADS + 2, :], lax.rem(HD - 2 * shard, HD), 1)
     bias[0] = heads[: HEADS + 1, :2].T
     value_bias[...] = heads[HEADS + 1 :, :2]
+    for a, b in zip(refs[19:23], small_outs):
+        stores.start(a, b)
     for load, a, b in zip(loads.started, held, copied):
         load.wait()
         stores.start(a, b)
@@ -1179,20 +1221,21 @@
 
 def results(*arrays):
     *wholes, small = arrays
+    small_ones = [
+        jax.ShapeDtypeStruct((1, 24), f32),
+        jax.ShapeDtypeStruct((1, 24), f32),
+        jax.ShapeDtypeStruct((1, 2, HEADS + 1), f32),
+        jax.ShapeDtypeStruct((1, 2), f32),
+    ]
     return pl.pallas_call(
         results_kernel,
-        out_shape=[
-            *[jax.ShapeDtypeStruct(a.shape, a.dtype) for a in wholes],
-            jax.ShapeDtypeStruct((1, 24), f32),
-            jax.ShapeDtypeStruct((1, 24), f32),
-            jax.ShapeDtypeStruct((1, 2, HEADS + 1), f32),
-            jax.ShapeDtypeStruct((1, 2), f32),
-        ],
+        out_shape=[*[jax.ShapeDtypeStruct(a.shape, a.dtype) for a in wholes], *small_ones],
         in_specs=[ANY] * 7 + [VMEM],
-        out_specs=[ANY] * 7 + [VMEM] * 4,
+        out_specs=[ANY] * 11,
         scratch_shapes=[
-            *[pltpu.VMEM(a.shape, a.dtype) for a in wholes],
-            *[pltpu.SemaphoreType.DMA((7,))] * 2,
+            *[pltpu.VMEM(a.shape, a.dtype) for a in (*small_ones, *wholes)],
+            pltpu.SemaphoreType.DMA((7,)),
+            pltpu.SemaphoreType.DMA((11,)),
         ],
     )(*wholes, small)
 

time: 197 us -> 193 us (0.980)
  Pallas kernels: 192 us -> 189 us
    pallas_call x1, Pallas kernels: 67.1 us -> 62.3 us  [feed_forward(): pl.pallas_call(mlp_kernel, out_shape=[jax.ShapeDtypeStruct((TOK, D), f32)...]
where the time goes in v1:
time: 193 us; the launch traced here: 190 us
  Pallas kernels  189 us (98%)
    pallas_call x1, Pallas kernels, back(): pl.pallas_call(back_kernel, out_shape=results_of, in_specs=[SMEM] + [VMEM...  75.4 us
    pallas_call x1, Pallas kernels, feed_forward(): pl.pallas_call(mlp_kernel, out_shape=[jax.ShapeDtypeStruct((TOK, D), f32)...  62.3 us
    pallas_call x1, Pallas kernels, attend(): pl.pallas_call(attend_kernel, out_shape=[*state, jax.ShapeDtypeStruct((4,...  48.1 us

profile of v1, /device:TPU:1, one launch (start us, length us, event | category | flops | bytes accessed | tf_op | source)
XLA Modules:
  0.0 189.9 jit_solution(3931833788999048086)
XLA Ops:
  0.6 48.1 %shard_map.203 = (bf16[4,4,2,128,256]{4,3,2,1,0:T(8,128)(2,1)}, bf16[2,768,128]{2,1,0:T(8,128)(2,1)}, bf16[128,1536]{1,0:T(8,128)(2,1)}, f32[128,1536]{1,0:T(8,1...) custom-call(s32[4]{0:T(128)} %refs_0_.1, ...), custom_call_target="tpu_custom_call" | custom-call | tf_op jit(solution)/shard_map/pallas_call | solution.py:493
  48.7 62.3 %shard_map.204 = (f32[128,1536]{1,0:T(8,128)}, bf16[128,768]{1,0:T(8,128)(2,1)}, f32[1,1536]{1,0:T(1,128)}, bf16[384,640]{1,0:T(8,128)(2,1)}, f32[128,1536]{1,0:...) custom-call(f32[128,1536]{1,0:T(8,128)} %get-tuple-element.51.refs_0, ...), custom_call_target="tpu_custom_call" | custom-call | tf_op jit(solution)/shard_map/pallas_call | solution.py:706
  111.0 75.4 %shard_map.205 = (bf16[128,1536]{1,0:T(8,128)(2,1)}, bf16[128,1536]{1,0:T(8,128)(2,1)}, f32[24,4480]{1,0:T(8,128)}, f32[24,4480]{1,0:T(8,128)}, f32[24,4480]{1,0...) custom-call(s32[4]{0:T(128)} %refs_0_.1, f32[1,768]{1,0:T(1,128)} %get-tuple-element.50.refs_1_, ...), custom_call_target="tpu_custom_call" | custom-call | tf_op jit(solution)/shard_map/pallas_call | solution.py:1118
  186.4 3.2 %shard_map.206 = (bf16[128,1536]{1,0:T(8,128)(2,1)}, bf16[128,1536]{1,0:T(8,128)(2,1)}, f32[24,4480]{1,0:T(8,128)}, f32[24,4480]{1,0:T(8,128)}, f32[24,4480]{1,0...) custom-call(bf16[128,1536]{1,0:T(8,128)(2,1)} %get-tuple-element.70., ...), custom_call_target="tpu_custom_call" | custom-call | tf_op jit(solution)/shard_map/pallas_call | solution.py:1230

commit v2 on v1

--- a/solution.py
+++ b/solution.py
@@ -204,7 +204,7 @@
 
 def attend_kernel(
     lengths, x, gain, bias, freqs, og, w_qkv_hbm, w_out_hbm, w_gate_hbm, w_up_hbm,
-    kv_hbm, q_hbm, act_hbm, resid_hbm, exact_hbm, lse_hbm, rope_hbm, gate_hbm, up_hbm, og_all, al_all,
+    kv_hbm, q_hbm, aa_part, resid_hbm, exact_hbm, lse_hbm, rope_hbm, gate_hbm, up_hbm, og_all, al_all,
     stats, acc, low_acc, stats_in, acc_in, low_in, w_qkv, w_out, o, pa, pb,
     kv, q, act, resid, exact, lse, rope, gate_w, up_w, wide_gate, wide_up, send_sems, recv_sems, local_sems,
 ):
@@ -239,7 +239,7 @@
     mine[:, pl.ds(0, HD)] = turn(back[:, :HD]).astype(bf16)
     mine[:, pl.ds(HD, HD)] = back[:, HD:].astype(bf16)
     everyone_in()
-    kept_back.append(moves.start(act, act_hbm))
+    kept_back.append(moves.start(act, aa_part.at[y]))
     load_out = moves.start(w_out_hbm, w_out)
     copies = Copies(send_sems, recv_sems)
     rows_of_og = Rows(me, copies, og, og_all)
@@ -424,6 +424,8 @@
 
     pl.loop(0, 4)(two_arrive)
     rows_of_og.pass_on(2)
+    mine = rows_of_og.mine
+    aa_far = [copies.send(act.at[mine], aa_part.at[y, mine], ys[d]) for d in (1, 3, 2)]
     pl.loop(4, 6)(two_arrive)
     kept_back.append(moves.start(kv, kv_hbm))
     merge = [
@@ -472,7 +474,7 @@
     swap.wait_recv()
     resid[...] = x[...].astype(f32) + (pa[...].astype(f32) + pb[...].astype(f32))
     kept_back.append(moves.start(resid, resid_hbm))
-    for copy in al_moves.values():
+    for copy in (*aa_far, *al_moves.values()):
         copy.wait_recv()
     moves.finish(kept_back)
     copies.finish()
@@ -493,7 +495,9 @@
     return pl.pallas_call(
         attend_kernel,
         out_shape=[
-            *state,
+            *state[:2],
+            jax.ShapeDtypeStruct((4, TOK, D), bf16),
+            *state[3:],
             jax.ShapeDtypeStruct((4, 2, TOK, D), bf16),
             jax.ShapeDtypeStruct((4, TOK, HEADS * HD), bf16),
         ],
@@ -512,7 +516,7 @@
             *[pltpu.VMEM((TOK, D), bf16)] * 2,
             *[pltpu.VMEM(a.shape, a.dtype) for a in state],
             *[pltpu.VMEM((D, WINDOW), bf16)] * 2,
-            *sems(52),
+            *sems(55),
             pltpu.SemaphoreType.DMA((15,)),
         ],
         compiler_params=params(1),
@@ -520,7 +524,7 @@
 
 
 def mlp_kernel(*refs):
-    resid, gain, og, aa, w_out_hbm, og_hbm, gate_hbm, up_w_hbm, w_down_hbm = refs[:9]
+    resid, gain, og, w_out_hbm, og_hbm, gate_hbm, up_w_hbm, w_down_hbm, aa_part = refs[:9]
     back_hbm, grads_hbm, gains_hbm, gate_sum_hbm, near_hbm, far_hbm, up_hbm, down_hbm, aa_all = refs[9:18]
     wd, og_all, act_all, grad_hidden, hidden, ggp, gup, bk, dn, bk_core, dn_core, bk_sent, bk_in = refs[18:31]
     nb, rn, gate_terms, gate_in, gate_w, up_w, up_terms, down_terms, down_sum, dn_in, w_out = refs[31:42]
@@ -536,7 +540,6 @@
     units = pl.ds(pl.multiple_of((y * 2 + c) * UNITS, 16), UNITS)
     load_down, load_og = moves.start(w_down_hbm.at[units], wd), moves.start(og_hbm, og_all)
     load_out = moves.start(w_out_hbm, w_out)
-    kept_back.append(moves.start(aa, aa_all.at[y, c]))
     everyone_in()
     copies = Copies(send_sems, recv_sems)
     half = TOK // 2
@@ -610,6 +613,16 @@
     for copy in to_core[0]:
         copy.wait_recv()
     block(0)
+    n = me["n"]
+    mine = pl.ds(pl.multiple_of(half * n, half), half)
+    theirs = pl.ds(pl.multiple_of(half * (1 - n), half), half)
+    aa_near = [copies.send(aa_part.at[y], aa_all.at[y, c], partner)]
+    aa_across = {}
+    for d in (1, 3, 2):
+        yi = step(me, "y", d)
+        got, slot = aa_part.at[yi, mine], aa_all.at[yi, c, mine]
+        aa_across[d] = copies.send(got, slot, other)
+        aa_near.append(copies.send(got, slot, partner))
     for d in (3, 1, 2):
         hidden_back(d)
     relay = {}
@@ -620,9 +633,6 @@
             to_core[4 - d].append(copies.send(got, got, partner))
             if d == 1 + 2 * k:
                 relay[d] = copies.send(got, got, ys[d])
-    aa_rows = Rows(me, copies, aa, aa_all)
-    aa_rows.start(1, 3, 2)
-    aa_rows.pair()
     for copy in to_core[3]:
         copy.wait_recv()
     block(3, 0)
@@ -648,13 +658,16 @@
         d: copies.send(gate_terms.at[:, z_cols(d)], gate_in.at[d - 1], zs[d]) for d in (1, 3, 2)
     }
     pass_block(2)
-    aa_rows.pass_on(1, 3, 2)
     for d in (1, 3, 2, 0):
         down_block(d)
     up_terms[...] = tn(gup[...].reshape(all_units), act_all[...].reshape(everything)).astype(bf16)
     kept_back.append(moves.start(up_terms, up_hbm))
     for d in range(4):
         sum_down(d)
+    dn_moves = {
+        d: copies.send(down_sum.at[step(me, "y", d)], dn_in.at[d // 2], ys[d]) for d in (1, 3)
+    }
+    kept_back.append(moves.start(down_sum.at[step(me, "y", 2)], far_hbm))
     swaps_back = []
     for k, rows in enumerate((low, high)):
         back = bk_sent[y, rows].astype(f32)
@@ -663,16 +676,15 @@
             back = back + bk_in[d - 1, rows].astype(f32)
         nb[rows] = back.astype(bf16)
         swaps_back.append(copies.send(nb.at[rows], rn.at[rows], other))
-    dn_moves = {
-        d: copies.send(down_sum.at[step(me, "y", d)], dn_in.at[d // 2], ys[d]) for d in (1, 3)
-    }
-    kept_back.append(moves.start(down_sum.at[step(me, "y", 2)], far_hbm))
     for zi in range(4):
         columns = og_all[:, :, :, pl.ds(384 * zi, 384)].reshape(GROUP * TOK, 384)
         sums = whole_tiles(tn(columns, hidden[...].reshape(all_units)).astype(bf16))
         down_terms[zi] = sums.reshape(4, 2, 48, COLUMNS)
     kept_back.append(moves.start(down_terms, down_hbm))
-    aa_rows.complete(1, 3, 2)
+    for d in (1, 3, 2):
+        aa_across[d].wait_recv()
+        got = aa_all.at[step(me, "y", d), c, theirs]
+        aa_near.append(copies.send(got, got, partner))
     for copy in swaps_back:
         copy.wait_recv()
     grad_act = nb[...].astype(f32) + rn[...].astype(f32)
@@ -696,7 +708,8 @@
         total = total + dn_in[d // 2].astype(f32)
     down_near[...] = total
     kept_back.append(moves.start(down_near, near_hbm))
-    aa_rows.wait()
+    for copy in aa_near:
+        copy.wait_recv()
     moves.finish(kept_back)
     copies.finish()
 
@@ -716,7 +729,7 @@
             jax.ShapeDtypeStruct((4, 4, 2, 48, COLUMNS), bf16),
             jax.ShapeDtypeStruct((4, 2, TOK, D), bf16),
         ],
-        in_specs=[VMEM] * 4 + [ANY] * 5,
+        in_specs=[VMEM] * 3 + [ANY] * 6,
         out_specs=[ANY] * 9,
         scratch_shapes=[
             pltpu.VMEM((UNITS, D), bf16),
@@ -742,8 +755,8 @@
             pltpu.VMEM((1, D), f32),
             pltpu.VMEM((D // 4, COLUMNS), bf16),
             pltpu.VMEM((TOK, D), f32),
-            *sems(48),
-            pltpu.SemaphoreType.DMA((14,)),
+            *sems(45),
+            pltpu.SemaphoreType.DMA((13,)),
         ],
         compiler_params=params(2),
     )(*arrays)
@@ -752,15 +765,15 @@
 def back_kernel(*refs):
     lengths, lse, grad_resid, grads_in, gain, mlp_gain_terms = refs[:6]
     x_hbm, rope_hbm, gate_sum, down_far, q_hbm, kv_hbm, exact_hbm, resid_hbm, near_hbm = refs[6:15]
-    al_hbm, w_qkv_hbm, act_hbm, up_terms, wd_terms = refs[15:20]
-    results_hbm = refs[20:28]
-    (g, stats, acc, acc_in, dkv, r1a, r1b, ta, tb, r2a, r2b, u, r3, w_qkv, act_all, gbt, gbt_all, al_all) = refs[28:46]
-    gp, gp_flat, gp_all, part, part_other, small, e1, e2, e3, f1, f2 = refs[46:57]
-    up_own, up_in, up_mid, wd_own, wd_across, wd_sum, wd_in, wd_mid, wd_second = refs[57:66]
-    gate_second, up_second = refs[66:68]
-    summed, third_in = refs[68:71], refs[71:74]
-    q_terms, q_first, q_mid, q_second, q_summed, q_third = refs[74:80]
-    down_in, down_part, down_other, q, kv, exact, resid, down_near, o_half, o_core, o_sum, o_in, o_mid, o_across, o_fin, o_third, *refs = refs[80:]
+    al_hbm, w_qkv_hbm, act_hbm, up_terms, wd_terms, aa_part = refs[15:21]
+    results_hbm = refs[21:29]
+    (g, stats, acc, acc_in, dkv, r1a, r1b, ta, tb, r2a, r2b, u, r3, w_qkv, act_all, gbt, gbt_all, al_all) = refs[29:47]
+    gp, gp_flat, gp_all, part, part_other, small, e1, e2, e3, f1, f2 = refs[47:58]
+    up_own, up_in, up_mid, wd_own, wd_across, wd_sum, wd_in, wd_mid, wd_second = refs[58:67]
+    gate_second, up_second = refs[67:69]
+    summed, third_in = refs[69:72], refs[72:75]
+    q_terms, q_first, q_mid, q_second, q_summed, q_third = refs[75:81]
+    down_in, down_part, down_other, q, kv, exact, resid, down_near, o_half, o_core, o_sum, o_in, o_mid, o_across, o_fin, o_third, *refs = refs[81:]
     x, rope, in_grad, layer_out, sum_gate, sum_up, sum_down, sum_qkv, sum_out, small_out, *refs = refs
     send_sems, recv_sems, local_sems = refs
 
@@ -863,7 +876,13 @@
 
     load_al = load(al_hbm, al_all)
     load_w = load(w_qkv_hbm, w_qkv)
-    load_act = load(act_hbm, act_all)
+    mine = pl.ds(pl.multiple_of(half * n, half), half)
+    theirs = pl.ds(pl.multiple_of(half * (1 - n), half), half)
+    load_act = [load(aa_part.at[y], act_all.at[y, c]), load(act_hbm.at[:, 1 - c], act_all.at[:, 1 - c])]
+    for d in (1, 2, 3):
+        yi = step(me, "y", d)
+        load_act.append(load(aa_part.at[yi, mine], act_all.at[yi, c, mine]))
+        load_act.append(load(act_hbm.at[yi, c, theirs], act_all.at[yi, c, theirs]))
     load_up = load(up_terms.at[:, z_cols(0)], up_own)
     load_wd = load(wd_terms.at[:, :, xh], wd_own)
 
@@ -976,13 +995,14 @@
     u[:, low] = ua.astype(bf16)
     u[:, high] = ub.astype(bf16)
     kv_last = copies.send(u.at[1 - xh], r3, across)
+    o_move.wait_recv()
+    o_sum[...] = (o_half[c].astype(f32) + o_core[...].astype(f32)).astype(bf16)
+    o_first = {d: copies.send(o_sum.at[step(me, "z", d)], o_in.at[d - 1], zs[d]) for d in (1, 3, 2)}
     load_wd.wait()
     wd_move.wait_recv()
     for zi in range(4):
         wd_sum[zi] = (wd_own[zi].astype(f32) + wd_across[zi].astype(f32)).astype(bf16)
     wd_first = {d: copies.send(wd_sum.at[step(me, "z", d)], wd_in.at[d - 1], zs[d]) for d in (1, 3, 2)}
-    o_move.wait_recv()
-    o_sum[...] = (o_half[c].astype(f32) + o_core[...].astype(f32)).astype(bf16)
     queries_back.wait_recv()
     load_rope.wait()
     load_x.wait()
@@ -1027,7 +1047,8 @@
     send_mid(1, up_own[...].astype(f32) + three(up_in), up_mid, up_second)
     load_strip.wait()
     collect(0)
-    load_act.wait()
+    for copy in load_act:
+        copy.wait()
     for copy in gp_moves:
         copy.wait_recv()
     q_terms[...] = tn(
@@ -1035,7 +1056,6 @@
     ).astype(bf16)
 
     q_one = {d: copies.send(q_terms.at[:, z_cols(d)], q_first.at[d - 1], zs[d]) for d in (1, 3, 2)}
-    o_first = {d: copies.send(o_sum.at[step(me, "z", d)], o_in.at[d - 1], zs[d]) for d in (1, 3, 2)}
     down_swap.wait_recv()
     load_resid.wait()
     layer_out[...] = (
@@ -1118,7 +1138,7 @@
     return pl.pallas_call(
         back_kernel,
         out_shape=results_of,
-        in_specs=[SMEM] + [VMEM] * 5 + [ANY] * 14,
+        in_specs=[SMEM] + [VMEM] * 5 + [ANY] * 15,
         out_specs=[ANY] * 8,
         scratch_shapes=[
             pltpu.VMEM((2, NQ, HD), bf16),
@@ -1184,7 +1204,7 @@
             pltpu.VMEM((2, TOK, HD), f32),
             *[pltpu.VMEM(a.shape, a.dtype) for a in results_of],
             *sems(93),
-            pltpu.SemaphoreType.DMA((21,)),
+            pltpu.SemaphoreType.DMA((28,)),
         ],
         compiler_params=params(9, 62),
     )(*arrays)
@@ -1246,18 +1266,19 @@
     half = HD // 2
     freqs = np.float32(rope_base) ** (-2.0 * np.arange(half, dtype=np.float32) / HD)
     freqs = np.concatenate([freqs, freqs]).astype(np.float32)[None]
-    kv, queries, act_attn, resid, exact, lse, rope, gate_w, up_w, out_grad_all, low_all = attend(
+    kv, queries, act_part, resid, exact, lse, rope, gate_w, up_w, out_grad_all, low_all = attend(
         lengths, layer_in, norm_attn, qkv_bias, freqs, out_grad, w_qkv, w_out, w_gate, w_up
     )
     (
         grad_resid, grads, gain_terms, gate_sum, down_near, down_far,
         up_terms, down_terms, act_attn_all,
     ) = feed_forward(
-        resid, norm_mlp, out_grad, act_attn, w_out, out_grad_all, gate_w, up_w, w_down
+        resid, norm_mlp, out_grad, w_out, out_grad_all, gate_w, up_w, w_down, act_part
     )
     sums = back(
         lengths, lse, grad_resid, grads, norm_attn, gain_terms, layer_in, rope, gate_sum, down_far,
         queries, kv, exact, resid, down_near, low_all, w_qkv, act_attn_all, up_terms, down_terms,
+        act_part,
     )
     in_grad, layer_out, sum_gate, sum_up, sum_down, sum_qkv, sum_out, *rest = results(*sums)
     sum_norm_attn, sum_norm_mlp, bias, value_bias = rest

time: 193 us -> 190 us (0.984)
  Pallas kernels: 189 us -> 185 us
    pallas_call x1, Pallas kernels: 75.4 us -> 72.8 us  [back(): pl.pallas_call(back_kernel, out_shape=results_of, in_specs=[SMEM] + [VMEM...]
where the time goes in v2:
time: 190 us; the launch traced here: 186 us
  Pallas kernels  185 us (97%)
    pallas_call x1, Pallas kernels, back(): pl.pallas_call(back_kernel, out_shape=results_of, in_specs=[SMEM] + [VMEM...  72.8 us
    pallas_call x1, Pallas kernels, feed_forward(): pl.pallas_call(mlp_kernel, out_shape=[jax.ShapeDtypeStruct((TOK, D), f32)...  60.8 us
    pallas_call x1, Pallas kernels, attend(): pl.pallas_call(attend_kernel, out_shape=[*state[:2], jax.ShapeDtypeStruct...  48.6 us

profile of v2, /device:TPU:1, one launch (start us, length us, event | category | flops | bytes accessed | tf_op | source)
XLA Modules:
  0.0 186.4 jit_solution(14723930419943679868)
XLA Ops:
  0.6 48.6 %shard_map.203 = (bf16[4,4,2,128,256]{4,3,2,1,0:T(8,128)(2,1)}, bf16[2,768,128]{2,1,0:T(8,128)(2,1)}, bf16[4,128,1536]{2,1,0:T(8,128)(2,1)}, f32[128,1536]{1,0:T...) custom-call(s32[4]{0:T(128)} %refs_0_.1, ...), custom_call_target="tpu_custom_call" | custom-call | tf_op jit(solution)/shard_map/pallas_call | solution.py:495
  49.3 60.8 %shard_map.204 = (f32[128,1536]{1,0:T(8,128)}, bf16[128,768]{1,0:T(8,128)(2,1)}, f32[1,1536]{1,0:T(1,128)}, bf16[384,640]{1,0:T(8,128)(2,1)}, f32[128,1536]{1,0:...) custom-call(f32[128,1536]{1,0:T(8,128)} %get-tuple-element.51.refs_0, ...), custom_call_target="tpu_custom_call" | custom-call | tf_op jit(solution)/shard_map/pallas_call | solution.py:719
  110.0 72.8 %shard_map.205 = (bf16[128,1536]{1,0:T(8,128)(2,1)}, bf16[128,1536]{1,0:T(8,128)(2,1)}, f32[24,4480]{1,0:T(8,128)}, f32[24,4480]{1,0:T(8,128)}, f32[24,4480]{1,0...) custom-call(s32[4]{0:T(128)} %refs_0_.1, f32[1,768]{1,0:T(1,128)} %get-tuple-element.50.refs_1_, ...), custom_call_target="tpu_custom_call" | custom-call | tf_op jit(solution)/shard_map/pallas_call | solution.py:1138
  182.9 3.2 %shard_map.206 = (bf16[128,1536]{1,0:T(8,128)(2,1)}, bf16[128,1536]{1,0:T(8,128)(2,1)}, f32[24,4480]{1,0:T(8,128)}, f32[24,4480]{1,0:T(8,128)}, f32[24,4480]{1,0...) custom-call(bf16[128,1536]{1,0:T(8,128)(2,1)} %get-tuple-element.70., ...), custom_call_target="tpu_custom_call" | custom-call | tf_op jit(solution)/shard_map/pallas_call | solution.py:1250

commit v3 on v2

--- a/solution.py
+++ b/solution.py
@@ -1056,12 +1056,19 @@
     ).astype(bf16)
 
     q_one = {d: copies.send(q_terms.at[:, z_cols(d)], q_first.at[d - 1], zs[d]) for d in (1, 3, 2)}
+    for d in (1, 3, 2):
+        o_first[d].wait_recv()
+    o_total = (o_sum[z].astype(f32) + three(o_in)).astype(bf16)
+    o_mid[0], o_mid[1] = o_total[:48], o_total[48:]
+    o_last = copies.send(o_mid.at[1 - xh], o_across, across)
     down_swap.wait_recv()
     load_resid.wait()
     layer_out[...] = (
         resid[...] + (down_part[...].astype(f32) + down_other[...].astype(f32))
     ).astype(bf16)
     keep_result(1, layer_out)
+    deliver(0)
+    keep_result(2, sum_gate)
     swap.wait_recv()
     grad_act = part[...].astype(f32) + part_other[...].astype(f32)
     rows = x[...].astype(f32)
@@ -1084,11 +1091,6 @@
         q_one[d].wait_recv()
     send_mid(3, q_terms[:, z_cols(0)].astype(f32) + three(q_first), q_mid, q_second)
     for d in (1, 3, 2):
-        o_first[d].wait_recv()
-    o_total = (o_sum[z].astype(f32) + three(o_in)).astype(bf16)
-    o_mid[0], o_mid[1] = o_total[:48], o_total[48:]
-    o_last = copies.send(o_mid.at[1 - xh], o_across, across)
-    for d in (1, 3, 2):
         small_one[d].wait_recv()
     f1[...] = small[...] + three(e1)
     small_two = {m: copies.send(f1, e2.at[k], near[m]) for k, m in enumerate(near_moves)}
@@ -1096,8 +1098,6 @@
     o_fin[...] = o_mid[xh].astype(f32) + o_across[...].astype(f32)
     o_end = copies.send(o_fin.at[give], o_third, partner)
     collect(1)
-    deliver(0)
-    keep_result(2, sum_gate)
     deliver(1)
     keep_result(3, sum_up)
     collect(2)

time: 190 us -> 189 us (level)
  no operation moved by 1% of the time
where the time goes in v3:
time: 189 us; the launch traced here: 186 us
  Pallas kernels  185 us (98%)
    pallas_call x1, Pallas kernels, back(): pl.pallas_call(back_kernel, out_shape=results_of, in_specs=[SMEM] + [VMEM...  72.2 us
    pallas_call x1, Pallas kernels, feed_forward(): pl.pallas_call(mlp_kernel, out_shape=[jax.ShapeDtypeStruct((TOK, D), f32)...  60.8 us
    pallas_call x1, Pallas kernels, attend(): pl.pallas_call(attend_kernel, out_shape=[*state[:2], jax.ShapeDtypeStruct...  48.6 us

profile of v3, /device:TPU:1, one launch (start us, length us, event | category | flops | bytes accessed | tf_op | source)
XLA Modules:
  0.0 185.8 jit_solution(3610670318738030467)
XLA Ops:
  0.6 48.6 %shard_map.203 = (bf16[4,4,2,128,256]{4,3,2,1,0:T(8,128)(2,1)}, bf16[2,768,128]{2,1,0:T(8,128)(2,1)}, bf16[4,128,1536]{2,1,0:T(8,128)(2,1)}, f32[128,1536]{1,0:T...) custom-call(s32[4]{0:T(128)} %refs_0_.1, ...), custom_call_target="tpu_custom_call" | custom-call | tf_op jit(solution)/shard_map/pallas_call | solution.py:495
  49.3 60.8 %shard_map.204 = (f32[128,1536]{1,0:T(8,128)}, bf16[128,768]{1,0:T(8,128)(2,1)}, f32[1,1536]{1,0:T(1,128)}, bf16[384,640]{1,0:T(8,128)(2,1)}, f32[128,1536]{1,0:...) custom-call(f32[128,1536]{1,0:T(8,128)} %get-tuple-element.51.refs_0, ...), custom_call_target="tpu_custom_call" | custom-call | tf_op jit(solution)/shard_map/pallas_call | solution.py:719
  110.0 72.2 %shard_map.205 = (bf16[128,1536]{1,0:T(8,128)(2,1)}, bf16[128,1536]{1,0:T(8,128)(2,1)}, f32[24,4480]{1,0:T(8,128)}, f32[24,4480]{1,0:T(8,128)}, f32[24,4480]{1,0...) custom-call(s32[4]{0:T(128)} %refs_0_.1, f32[1,768]{1,0:T(1,128)} %get-tuple-element.50.refs_1_, ...), custom_call_target="tpu_custom_call" | custom-call | tf_op jit(solution)/shard_map/pallas_call | solution.py:1138
  182.3 3.2 %shard_map.206 = (bf16[128,1536]{1,0:T(8,128)(2,1)}, bf16[128,1536]{1,0:T(8,128)(2,1)}, f32[24,4480]{1,0:T(8,128)}, f32[24,4480]{1,0:T(8,128)}, f32[24,4480]{1,0...) custom-call(bf16[128,1536]{1,0:T(8,128)(2,1)} %get-tuple-element.70., ...), custom_call_target="tpu_custom_call" | custom-call | tf_op jit(solution)/shard_map/pallas_call | solution.py:1250
